TPU v7x, 128 devices: a whole 4x4x4 slice. The times are simulated.
128 devices in a mesh: section: 4 (over z_lo, core), expert: 32 (over y, z_hi, x).
Axes of the slice: x: 4, y: 4, z: 4 (z_hi: 2, z_lo: 2; z = z_hi * 2 + z_lo), core: 2. Of those that a mesh axis runs over, the one named last changes fastest.
Arguments:
- tokens: bfloat16 [8, 512, 2048], P(None, 'expert'), may hold values from -6 to 6
- cotangent: bfloat16 [8, 512, 2048], P(None, 'expert'), may hold values from -6 to 6
- reward_weight: float32 [8, 512], P(None, 'expert'), may hold values from 0.2 to 14, as said below
- routes: int32 [4, 8, 512, 8], P('section', None, 'expert'), may hold values from 0 to 31, all different within a row; in each aligned block of 16 rows (0 to 15, 16 to 31, ..., all dimensions but the last counted through in order) at most 5 rows name the same one
- combine: float32 [4, 8, 512, 8], P('section', None, 'expert'), may hold values from 0.05 to 0.25
- w_up: bfloat16 [4, 32, 2048, 768], P('section', 'expert'), may hold values from -0.125 to 0.125
- w_down: bfloat16 [4, 32, 768, 2048], P('section', 'expert'), may hold values from -0.21875 to 0.21875
Outputs:
- layer_out: bfloat16 [4, 8, 512, 2048], P('section', None, 'expert')
- input_grad: bfloat16 [4, 8, 512, 2048], P('section', None, 'expert')
- grad_up: bfloat16 [4, 32, 2048, 768], P('section', 'expert')
Inputs may be any that keep to these rules, and one draw needn't show every extreme that they name: `routes`: each row names 8 different experts. Within the 16 rows of one device for one layer and micro-batch, no expert is named more than 5 times. `reward_weight`: Positive.
All inputs are finite; a program needn't handle non-finite values.
Results may differ from a plain program's by a relative error of at most 0.018.
Values may be sent and summed in bfloat16 or wider, within the bound.
A program may use at most 192 MiB of HBM per device.

v0:
```python
import jax
import jax.numpy as jnp
from jax import lax
from jax.sharding import PartitionSpec as P

EPS = 1e-06


def shifted(value, axis, by):
    peers = lax.axis_size(axis)
    pairs = [(i, i + by) for i in range(peers) if 0 <= i + by < peers]
    return lax.ppermute(value, axis, pairs)


def rms_forward(inputs):
    values = inputs.astype(jnp.float32)
    scale = lax.rsqrt(jnp.mean(values * values, axis=-1, keepdims=True) + EPS)
    return values * scale


def rms_backward(inputs, grad):
    values = inputs.astype(jnp.float32)
    scale = lax.rsqrt(jnp.mean(values * values, axis=-1, keepdims=True) + EPS)
    inner = jnp.mean(grad * values, axis=-1, keepdims=True)
    return scale * grad - values * (scale * scale * scale) * inner


def silu_slope(pre):
    sigma = jax.nn.sigmoid(pre)
    return sigma * (1.0 + pre * (1.0 - sigma))


def slot_table(route, experts, capacity):
    flat = route.reshape(-1)
    onehot = (flat[:, None] == jnp.arange(experts, dtype=jnp.int32)[None, :]).astype(jnp.int32)
    before = jnp.cumsum(onehot, axis=0) - onehot
    rank = jnp.sum(before * onehot, axis=1)
    return flat * capacity + rank


def put_slice(store, value, safe, valid):
    older = lax.dynamic_index_in_dim(store, safe, 0, keepdims=False)
    return lax.dynamic_update_index_in_dim(store, jnp.where(valid, value, older), safe, 0)


def shards(tokens, cotangent, reward_weight, routes, combine, w_up, w_down):
    sections = lax.axis_size("section")
    my_section = lax.axis_index("section")
    width = lax.axis_size("expert")
    micro, tok_dev, model = tokens.shape
    top = routes.shape[-1]
    exp_dev = w_up.shape[1]
    hidden = w_up.shape[-1]
    experts = exp_dev * width
    capacity = max(2, 5 * tok_dev * top // (4 * experts))
    up_local = w_up[0]
    down_local = w_down[0]
    pair_token = jnp.arange(tok_dev * top, dtype=jnp.int32) // top
    ticks = micro + sections - 1

    def scatter_rows(rows, slot):
        empty = jnp.zeros((experts * capacity, model), jnp.bfloat16)
        return empty.at[slot].set(rows).reshape(width, exp_dev * capacity, model)

    def expert_pre(received):
        blocks = received.reshape(width, exp_dev, capacity, model)
        pre = jnp.einsum("sjcd,jdf->sjcf", blocks, up_local, preferred_element_type=jnp.float32)
        return (blocks, pre)

    zero_blocks = jnp.zeros((width, exp_dev, capacity, model), jnp.bfloat16)
    zero_pre = jnp.zeros((width, exp_dev, capacity, hidden), jnp.float32)
    zero_grad_pre = jnp.zeros((width, exp_dev, capacity, hidden), jnp.bfloat16)

    def expert_forward(received):
        blocks, pre = expert_pre(received)
        act = jax.nn.silu(pre).astype(jnp.bfloat16)
        result = jnp.einsum(
            "sjcf,jfd->sjcd", act, down_local, preferred_element_type=jnp.float32
        ).astype(jnp.bfloat16)
        return (result, blocks, pre)

    stash_in = jnp.zeros((micro, tok_dev, model), jnp.bfloat16)
    layer_out = jnp.zeros((micro, tok_dev, model), jnp.bfloat16)
    stash_rows = jnp.zeros((micro, width, exp_dev, capacity, model), jnp.bfloat16)
    stash_pre = jnp.zeros((micro, width, exp_dev, capacity, hidden), jnp.float32)
    incoming = jnp.zeros((tok_dev, model), jnp.bfloat16)
    for tick in range(ticks):
        index = tick - my_section
        valid = (index >= 0) & (index < micro)
        safe = jnp.clip(index, 0, micro - 1)
        first = lax.dynamic_index_in_dim(tokens, safe, 0, keepdims=False)
        x_in = jnp.where(my_section == 0, first, incoming)
        route = lax.dynamic_index_in_dim(routes[0], safe, 0, keepdims=False)
        coef = lax.dynamic_index_in_dim(combine[0], safe, 0, keepdims=False)
        normed = rms_forward(x_in).astype(jnp.bfloat16)
        slot = slot_table(route, experts, capacity)
        sent = jnp.where(
            valid,
            scatter_rows(normed[pair_token], slot),
            jnp.zeros((width, exp_dev * capacity, model), jnp.bfloat16),
        )
        received = lax.all_to_all(sent, "expert", split_axis=0, concat_axis=0, tiled=True)
        result, blocks, pre = lax.cond(
            valid, lambda: expert_forward(received), lambda: (zero_blocks, zero_blocks, zero_pre)
        )
        returned = lax.all_to_all(
            result.reshape(width, exp_dev * capacity, model),
            "expert",
            split_axis=0,
            concat_axis=0,
            tiled=True,
        )
        rows = returned.reshape(experts * capacity, model)[slot].astype(jnp.float32)
        mixed = (rows * coef.reshape(-1)[:, None]).reshape(tok_dev, top, model).sum(axis=1)
        out = (x_in.astype(jnp.float32) + mixed).astype(jnp.bfloat16)
        out = jnp.where(valid, out, x_in)
        layer_out = put_slice(layer_out, out, safe, valid)
        stash_in = put_slice(stash_in, x_in, safe, valid)
        stash_rows = put_slice(stash_rows, blocks, safe, valid)
        stash_pre = put_slice(stash_pre, pre, safe, valid)
        if tick + 1 < ticks:
            incoming = shifted(out, "section", 1)
    local_total = jnp.sum(reward_weight)
    total = lax.psum(local_total, "expert")
    factor = reward_weight * (micro * tok_dev * width / total)
    top_grad = (cotangent.astype(jnp.float32) * factor[..., None]).astype(jnp.bfloat16)
    input_grad = jnp.zeros((micro, tok_dev, model), jnp.bfloat16)
    kept_grad_pre = jnp.zeros((micro, width, exp_dev, capacity, hidden), jnp.bfloat16)
    from_next = jnp.zeros((tok_dev, model), jnp.bfloat16)
    zero_send = jnp.zeros((width, exp_dev * capacity, model), jnp.bfloat16)
    for tick in range(ticks):
        index = tick - (sections - 1 - my_section)
        valid = (index >= 0) & (index < micro)
        safe = jnp.clip(index, 0, micro - 1)
        last = lax.dynamic_index_in_dim(top_grad, safe, 0, keepdims=False)
        g_in = jnp.where(my_section == sections - 1, last, from_next)
        x_in = lax.dynamic_index_in_dim(stash_in, safe, 0, keepdims=False)
        route = lax.dynamic_index_in_dim(routes[0], safe, 0, keepdims=False)
        coef = lax.dynamic_index_in_dim(combine[0], safe, 0, keepdims=False)
        slot = slot_table(route, experts, capacity)
        scaled = (g_in.astype(jnp.float32)[pair_token] * coef.reshape(-1)[:, None]).astype(
            jnp.bfloat16
        )
        grads_sent = jnp.where(valid, scatter_rows(scaled, slot), zero_send)
        kept_pre = lax.dynamic_index_in_dim(stash_pre, safe, 0, keepdims=False)
        grads_got = lax.all_to_all(grads_sent, "expert", split_axis=0, concat_axis=0, tiled=True)

        def expert_backward():
            grads_blocks = grads_got.reshape(width, exp_dev, capacity, model)
            grad_act = jnp.einsum(
                "sjcd,jfd->sjcf", grads_blocks, down_local, preferred_element_type=jnp.float32
            )
            grad_pre = (grad_act * silu_slope(kept_pre)).astype(jnp.bfloat16)
            grad_rows = jnp.einsum(
                "sjcf,jdf->sjcd", grad_pre, up_local, preferred_element_type=jnp.float32
            ).astype(jnp.bfloat16)
            return (grad_rows.reshape(width, exp_dev * capacity, model), grad_pre)

        grad_rows, grad_pre = lax.cond(valid, expert_backward, lambda: (zero_send, zero_grad_pre))
        kept_grad_pre = put_slice(kept_grad_pre, grad_pre, safe, valid)
        back = lax.all_to_all(grad_rows, "expert", split_axis=0, concat_axis=0, tiled=True)
        gathered = back.reshape(experts * capacity, model)[slot].astype(jnp.float32)
        grad_normed = gathered.reshape(tok_dev, top, model).sum(axis=1)
        grad_x = (g_in.astype(jnp.float32) + rms_backward(x_in, grad_normed)).astype(jnp.bfloat16)
        grad_x = jnp.where(valid, grad_x, g_in)
        input_grad = put_slice(input_grad, grad_x, safe, valid)
        if tick + 1 < ticks:
            from_next = shifted(grad_x, "section", -1)
    grad_acc = jnp.einsum(
        "msjcd,msjcf->jdf", stash_rows, kept_grad_pre, preferred_element_type=jnp.float32
    )
    return (layer_out[None], input_grad[None], grad_acc.astype(jnp.bfloat16)[None])


def solution(mesh):
    return jax.shard_map(
        shards,
        mesh=mesh,
        in_specs=(
            P(None, "expert", None),
            P(None, "expert", None),
            P(None, "expert"),
            P("section", None, "expert", None),
            P("section", None, "expert", None),
            P("section", "expert", None, None),
            P("section", "expert", None, None),
        ),
        out_specs=(
            P("section", None, "expert", None),
            P("section", None, "expert", None),
            P("section", "expert", None, None),
        ),
        check_vma=False,
    )
```

profile of v0, /device:TPU:0, one launch (start us, length us, event | category | flops | bytes accessed | tf_op | source)
XLA Modules:
  0.0 1728.0 jit_solution(15044954386091978891)
XLA Ops:
  9.2 10.8 all-to-all-start
  43.4 96.9 %psum.7 = f32[]{:T(128)} all-reduce(f32[]{:T(128)} %reduce_sum.795), channel_id=1, replica_groups=mesh['section'=4,'expert'=32] {'expert'}, use_global_device_ids=true, to_apply=%region_78.79 | all-reduce | flops 1 | bytes 8 | tf_op jit(solution)/shard_map/psum | solution.py:124
  194.4 11.7 all-to-all-done.1
  237.1 15.0 all-to-all-done.2
  252.1 7.3 conditional.23
  268.8 14.7 all-to-all-done.3
  312.6 15.1 all-to-all-done.4
  327.7 7.4 conditional.24
  343.7 15.1 all-to-all-done.5
  385.8 17.1 all-to-all-done.6
  402.9 7.4 conditional.25
  418.7 15.8 all-to-all-done.7
  460.7 17.9 %all-to-all-done.8 = bf16[32,5,2048]{2,1,0:T(8,128)(2,1)} async-done(((bf16[32,5,2048]{2,1,0:T(8,128)(2,1)}), bf16[32,5,2048]{2,1,0:T(8,128)(2,1)}, u32[]{:S(2)}, u32[]{:S(2)}) %all-to-all-start.8) | async-done | bytes 655392 | tf_op jit(solution)/shard_map/all_to_all | solution.py:102
  478.6 7.4 conditional.26
  494.2 15.9 all-to-all-done.9
  536.1 17.1 all-to-all-done.10
  553.2 7.3 conditional.27
  569.3 15.9 all-to-all-done.11
  612.8 15.4 all-to-all-done.12
  628.2 7.3 conditional.28
  645.2 14.6 all-to-all-done.13
  690.7 13.2 all-to-all-done.14
  703.9 7.4 conditional.29
  754.6 9.9 all-to-all-start.16
  769.5 14.2 all-to-all-done.16
  798.3 10.2 all-to-all-done.17
  841.6 13.4 all-to-all-done.18
  869.2 11.8 all-to-all-done.19
  910.4 12.7 all-to-all-done.20
  936.0 10.9 all-to-all-done.22
  955.2 17.0 all-to-all-done.23
  1001.2 15.7 all-to-all-done.24
  1026.2 15.7 all-to-all-done.25
  1071.2 9.5 all-to-all-done.26
  1091.2 10.8 all-to-all-done.27
  1115.0 10.7 collective-permute-done.12
  1143.1 9.7 all-to-all-done.28
  1152.8 6.6 conditional.36
  1168.8 10.8 all-to-all-done.29
  1192.5 7.3 collective-permute-done.13
  1217.2 9.7 all-to-all-done.30
  1226.9 6.6 conditional.37
  1242.8 10.8 all-to-all-done.31
  1266.7 9.4 collective-permute-done.14
  1293.4 9.7 all-to-all-done.32
  1303.1 6.6 conditional.38
  1319.0 10.8 all-to-all-done.33
  1342.8 9.3 collective-permute-done.15
  1369.8 9.8 all-to-all-done.34
  1406.3 8.8 all-to-all-start.21
  1428.1 10.2 collective-permute-done.16
  1446.8 9.7 all-to-all-start.36
  1470.6 6.6 conditional.40
  1484.7 12.6 all-to-all-done.37
  1509.7 6.7 collective-permute-done.17
  1533.3 10.8 all-to-all-done.38
  1544.1 6.8 conditional.41
  1560.6 10.5 all-to-all-done.39
  1583.7 9.5 collective-permute-done.18
  1611.7 9.3 all-to-all-done.40
  1638.1 11.3 all-to-all-done.41
  1687.9 8.2 all-to-all-done.42
  1696.0 6.6 conditional.43
  1711.1 9.1 fusion.429
  (989 shorter events, 1052.8 us)
Async XLA Ops:
  9.2 170.0 %all-to-all-start = ((bf16[32,5,2048]{2,1,0:T(8,128)(2,1)}), bf16[32,5,2048]{2,1,0:T(8,128)(2,1)}, u32[]{:S(2)}, u32[]{:S(2)}) async-start(bf16[32,5,2048]{2,1,0:T(8,128)(2,1)} %select_n.1396), calls=%async_computation | async-start | bytes 2097152 | tf_op jit(solution)/shard_map/all_to_all | solution.py:102
  187.2 18.9 %all-to-all-start.1 = ((bf16[32,5,2048]{2,1,0:T(8,128)(2,1)}), bf16[32,5,2048]{2,1,0:T(8,128)(2,1)}, u32[]{:S(2)}, u32[]{:S(2)}) async-start(bf16[32,5,2048]{2,1,0:T(8,128)(2,1)} %bitcast.1842), calls=%async_computation.1 | async-start | bytes 2097152 | tf_op jit(solution)/shard_map/all_to_all | solution.py:106
  214.1 2.2 collective-permute-start
  228.7 23.4 %all-to-all-start.2 = ((bf16[32,5,2048]{2,1,0:T(8,128)(2,1)}), bf16[32,5,2048]{2,1,0:T(8,128)(2,1)}, u32[]{:S(2)}, u32[]{:S(2)}) async-start(bf16[32,5,2048]{2,1,0:T(8,128)(2,1)} %select_n.1407), calls=%async_computation.2 | async-start | bytes 2097152 | tf_op jit(solution)/shard_map/all_to_all | solution.py:102
  260.7 22.8 %all-to-all-start.3 = ((bf16[32,5,2048]{2,1,0:T(8,128)(2,1)}), bf16[32,5,2048]{2,1,0:T(8,128)(2,1)}, u32[]{:S(2)}, u32[]{:S(2)}) async-start(bf16[32,5,2048]{2,1,0:T(8,128)(2,1)} %bitcast.1841), calls=%async_computation.3 | async-start | bytes 2097152 | tf_op jit(solution)/shard_map/all_to_all | solution.py:106
  292.3 2.6 collective-permute-start.1
  304.7 23.0 %all-to-all-start.4 = ((bf16[32,5,2048]{2,1,0:T(8,128)(2,1)}), bf16[32,5,2048]{2,1,0:T(8,128)(2,1)}, u32[]{:S(2)}, u32[]{:S(2)}) async-start(bf16[32,5,2048]{2,1,0:T(8,128)(2,1)} %select_n.1415), calls=%async_computation.4 | async-start | bytes 2097152 | tf_op jit(solution)/shard_map/all_to_all | solution.py:102
  336.4 22.5 %all-to-all-start.5 = ((bf16[32,5,2048]{2,1,0:T(8,128)(2,1)}), bf16[32,5,2048]{2,1,0:T(8,128)(2,1)}, u32[]{:S(2)}, u32[]{:S(2)}) async-start(bf16[32,5,2048]{2,1,0:T(8,128)(2,1)} %bitcast.1843), calls=%async_computation.5 | async-start | bytes 2097152 | tf_op jit(solution)/shard_map/all_to_all | solution.py:106
  367.4 2.2 collective-permute-start.2
  379.6 23.3 %all-to-all-start.6 = ((bf16[32,5,2048]{2,1,0:T(8,128)(2,1)}), bf16[32,5,2048]{2,1,0:T(8,128)(2,1)}, u32[]{:S(2)}, u32[]{:S(2)}) async-start(bf16[32,5,2048]{2,1,0:T(8,128)(2,1)} %select_n.1423), calls=%async_computation.6 | async-start | bytes 2097152 | tf_op jit(solution)/shard_map/all_to_all | solution.py:102
  411.6 22.9 %all-to-all-start.7 = ((bf16[32,5,2048]{2,1,0:T(8,128)(2,1)}), bf16[32,5,2048]{2,1,0:T(8,128)(2,1)}, u32[]{:S(2)}, u32[]{:S(2)}) async-start(bf16[32,5,2048]{2,1,0:T(8,128)(2,1)} %bitcast.1844), calls=%async_computation.7 | async-start | bytes 2097152 | tf_op jit(solution)/shard_map/all_to_all | solution.py:106
  443.1 2.2 collective-permute-start.3
  455.1 23.5 %all-to-all-start.8 = ((bf16[32,5,2048]{2,1,0:T(8,128)(2,1)}), bf16[32,5,2048]{2,1,0:T(8,128)(2,1)}, u32[]{:S(2)}, u32[]{:S(2)}) async-start(bf16[32,5,2048]{2,1,0:T(8,128)(2,1)} %select_n.1431), calls=%async_computation.8 | async-start | bytes 2097152 | tf_op jit(solution)/shard_map/all_to_all | solution.py:102
  487.3 22.8 %all-to-all-start.9 = ((bf16[32,5,2048]{2,1,0:T(8,128)(2,1)}), bf16[32,5,2048]{2,1,0:T(8,128)(2,1)}, u32[]{:S(2)}, u32[]{:S(2)}) async-start(bf16[32,5,2048]{2,1,0:T(8,128)(2,1)} %bitcast.1847), calls=%async_computation.9 | async-start | bytes 2097152 | tf_op jit(solution)/shard_map/all_to_all | solution.py:106
  517.9 2.2 collective-permute-start.4
  530.0 23.3 %all-to-all-start.10 = ((bf16[32,5,2048]{2,1,0:T(8,128)(2,1)}), bf16[32,5,2048]{2,1,0:T(8,128)(2,1)}, u32[]{:S(2)}, u32[]{:S(2)}) async-start(bf16[32,5,2048]{2,1,0:T(8,128)(2,1)} %select_n.1439), calls=%async_computation.10 | async-start | bytes 2097152 | tf_op jit(solution)/shard_map/all_to_all | solution.py:102
  561.9 23.2 %all-to-all-start.11 = ((bf16[32,5,2048]{2,1,0:T(8,128)(2,1)}), bf16[32,5,2048]{2,1,0:T(8,128)(2,1)}, u32[]{:S(2)}, u32[]{:S(2)}) async-start(bf16[32,5,2048]{2,1,0:T(8,128)(2,1)} %bitcast.1848), calls=%async_computation.11 | async-start | bytes 2097152 | tf_op jit(solution)/shard_map/all_to_all | solution.py:106
  592.9 2.2 collective-permute-start.5
  605.0 23.3 %all-to-all-start.12 = ((bf16[32,5,2048]{2,1,0:T(8,128)(2,1)}), bf16[32,5,2048]{2,1,0:T(8,128)(2,1)}, u32[]{:S(2)}, u32[]{:S(2)}) async-start(bf16[32,5,2048]{2,1,0:T(8,128)(2,1)} %select_n.1447), calls=%async_computation.12 | async-start | bytes 2097152 | tf_op jit(solution)/shard_map/all_to_all | solution.py:102
  636.9 22.8 %all-to-all-start.13 = ((bf16[32,5,2048]{2,1,0:T(8,128)(2,1)}), bf16[32,5,2048]{2,1,0:T(8,128)(2,1)}, u32[]{:S(2)}, u32[]{:S(2)}) async-start(bf16[32,5,2048]{2,1,0:T(8,128)(2,1)} %bitcast.1849), calls=%async_computation.13 | async-start | bytes 2097152 | tf_op jit(solution)/shard_map/all_to_all | solution.py:106
  668.5 2.3 collective-permute-start.6
  680.7 23.2 %all-to-all-start.14 = ((bf16[32,5,2048]{2,1,0:T(8,128)(2,1)}), bf16[32,5,2048]{2,1,0:T(8,128)(2,1)}, u32[]{:S(2)}, u32[]{:S(2)}) async-start(bf16[32,5,2048]{2,1,0:T(8,128)(2,1)} %select_n.1455), calls=%async_computation.14 | async-start | bytes 2097152 | tf_op jit(solution)/shard_map/all_to_all | solution.py:102
  712.7 23.0 %all-to-all-start.15 = ((bf16[32,5,2048]{2,1,0:T(8,128)(2,1)}), bf16[32,5,2048]{2,1,0:T(8,128)(2,1)}, u32[]{:S(2)}, u32[]{:S(2)}) async-start(bf16[32,5,2048]{2,1,0:T(8,128)(2,1)} %bitcast.1839), calls=%async_computation.15 | async-start | bytes 2097152 | tf_op jit(solution)/shard_map/all_to_all | solution.py:106
  743.6 2.2 collective-permute-start.7
  754.6 29.1 %all-to-all-start.16 = ((bf16[32,5,2048]{2,1,0:T(8,128)(2,1)}), bf16[32,5,2048]{2,1,0:T(8,128)(2,1)}, u32[]{:S(2)}, u32[]{:S(2)}) async-start(bf16[32,5,2048]{2,1,0:T(8,128)(2,1)} %select_n.1463), calls=%async_computation.16 | async-start | bytes 2097152 | tf_op jit(solution)/shard_map/all_to_all | solution.py:102
  786.9 21.7 %all-to-all-start.17 = ((bf16[32,5,2048]{2,1,0:T(8,128)(2,1)}), bf16[32,5,2048]{2,1,0:T(8,128)(2,1)}, u32[]{:S(2)}, u32[]{:S(2)}) async-start(bf16[32,5,2048]{2,1,0:T(8,128)(2,1)} %bitcast.1845), calls=%async_computation.17 | async-start | bytes 2097152 | tf_op jit(solution)/shard_map/all_to_all | solution.py:106
  816.4 6.4 collective-permute-start.8
  831.6 23.4 %all-to-all-start.18 = ((bf16[32,5,2048]{2,1,0:T(8,128)(2,1)}), bf16[32,5,2048]{2,1,0:T(8,128)(2,1)}, u32[]{:S(2)}, u32[]{:S(2)}) async-start(bf16[32,5,2048]{2,1,0:T(8,128)(2,1)} %select_n.1471), calls=%async_computation.18 | async-start | bytes 2097152 | tf_op jit(solution)/shard_map/all_to_all | solution.py:102
  858.1 22.9 %all-to-all-start.19 = ((bf16[32,5,2048]{2,1,0:T(8,128)(2,1)}), bf16[32,5,2048]{2,1,0:T(8,128)(2,1)}, u32[]{:S(2)}, u32[]{:S(2)}) async-start(bf16[32,5,2048]{2,1,0:T(8,128)(2,1)} %bitcast.1846), calls=%async_computation.19 | async-start | bytes 2097152 | tf_op jit(solution)/shard_map/all_to_all | solution.py:106
  888.9 2.3 collective-permute-start.9
  899.8 23.2 %all-to-all-start.20 = ((bf16[32,5,2048]{2,1,0:T(8,128)(2,1)}), bf16[32,5,2048]{2,1,0:T(8,128)(2,1)}, u32[]{:S(2)}, u32[]{:S(2)}) async-start(bf16[32,5,2048]{2,1,0:T(8,128)(2,1)} %select_n.1479), calls=%async_computation.20 | async-start | bytes 2097152 | tf_op jit(solution)/shard_map/all_to_all | solution.py:102
  923.1 23.8 %all-to-all-start.22 = ((bf16[32,5,2048]{2,1,0:T(8,128)(2,1)}), bf16[32,5,2048]{2,1,0:T(8,128)(2,1)}, u32[]{:S(2)}, u32[]{:S(2)}) async-start(bf16[32,5,2048]{2,1,0:T(8,128)(2,1)} %select_n.1500), calls=%async_computation.22 | async-start | bytes 2097152 | tf_op jit(solution)/shard_map/all_to_all | solution.py:146
  949.1 23.1 %all-to-all-start.23 = ((bf16[32,5,2048]{2,1,0:T(8,128)(2,1)}), bf16[32,5,2048]{2,1,0:T(8,128)(2,1)}, u32[]{:S(2)}, u32[]{:S(2)}) async-start(bf16[32,5,2048]{2,1,0:T(8,128)(2,1)} %copy.311), calls=%async_computation.23 | async-start | bytes 2097152 | tf_op jit(solution)/shard_map/all_to_all | solution.py:161
  982.4 3.1 collective-permute-start.10
  993.4 23.5 %all-to-all-start.24 = ((bf16[32,5,2048]{2,1,0:T(8,128)(2,1)}), bf16[32,5,2048]{2,1,0:T(8,128)(2,1)}, u32[]{:S(2)}, u32[]{:S(2)}) async-start(bf16[32,5,2048]{2,1,0:T(8,128)(2,1)} %select_n.1533), calls=%async_computation.24 | async-start | bytes 2097152 | tf_op jit(solution)/shard_map/all_to_all | solution.py:146
  1019.1 22.8 %all-to-all-start.25 = ((bf16[32,5,2048]{2,1,0:T(8,128)(2,1)}), bf16[32,5,2048]{2,1,0:T(8,128)(2,1)}, u32[]{:S(2)}, u32[]{:S(2)}) async-start(bf16[32,5,2048]{2,1,0:T(8,128)(2,1)} %copy.316), calls=%async_computation.25 | async-start | bytes 2097152 | tf_op jit(solution)/shard_map/all_to_all | solution.py:161
  1051.6 3.1 collective-permute-start.11
  1062.0 18.7 %all-to-all-start.26 = ((bf16[32,5,2048]{2,1,0:T(8,128)(2,1)}), bf16[32,5,2048]{2,1,0:T(8,128)(2,1)}, u32[]{:S(2)}, u32[]{:S(2)}) async-start(bf16[32,5,2048]{2,1,0:T(8,128)(2,1)} %select_n.1541), calls=%async_computation.26 | async-start | bytes 2097152 | tf_op jit(solution)/shard_map/all_to_all | solution.py:146
  1083.3 18.7 %all-to-all-start.27 = ((bf16[32,5,2048]{2,1,0:T(8,128)(2,1)}), bf16[32,5,2048]{2,1,0:T(8,128)(2,1)}, u32[]{:S(2)}, u32[]{:S(2)}) async-start(bf16[32,5,2048]{2,1,0:T(8,128)(2,1)} %copy.321), calls=%async_computation.27 | async-start | bytes 2097152 | tf_op jit(solution)/shard_map/all_to_all | solution.py:161
  1111.7 14.0 collective-permute-start.12
  1134.0 18.7 %all-to-all-start.28 = ((bf16[32,5,2048]{2,1,0:T(8,128)(2,1)}), bf16[32,5,2048]{2,1,0:T(8,128)(2,1)}, u32[]{:S(2)}, u32[]{:S(2)}) async-start(bf16[32,5,2048]{2,1,0:T(8,128)(2,1)} %select_n.1549), calls=%async_computation.28 | async-start | bytes 2097152 | tf_op jit(solution)/shard_map/all_to_all | solution.py:146
  1160.7 18.9 %all-to-all-start.29 = ((bf16[32,5,2048]{2,1,0:T(8,128)(2,1)}), bf16[32,5,2048]{2,1,0:T(8,128)(2,1)}, u32[]{:S(2)}, u32[]{:S(2)}) async-start(bf16[32,5,2048]{2,1,0:T(8,128)(2,1)} %copy.326), calls=%async_computation.29 | async-start | bytes 2097152 | tf_op jit(solution)/shard_map/all_to_all | solution.py:161
  1189.2 10.6 collective-permute-start.13
  1208.2 18.7 %all-to-all-start.30 = ((bf16[32,5,2048]{2,1,0:T(8,128)(2,1)}), bf16[32,5,2048]{2,1,0:T(8,128)(2,1)}, u32[]{:S(2)}, u32[]{:S(2)}) async-start(bf16[32,5,2048]{2,1,0:T(8,128)(2,1)} %select_n.1557), calls=%async_computation.30 | async-start | bytes 2097152 | tf_op jit(solution)/shard_map/all_to_all | solution.py:146
  1234.9 18.7 %all-to-all-start.31 = ((bf16[32,5,2048]{2,1,0:T(8,128)(2,1)}), bf16[32,5,2048]{2,1,0:T(8,128)(2,1)}, u32[]{:S(2)}, u32[]{:S(2)}) async-start(bf16[32,5,2048]{2,1,0:T(8,128)(2,1)} %copy.331), calls=%async_computation.31 | async-start | bytes 2097152 | tf_op jit(solution)/shard_map/all_to_all | solution.py:161
  1263.2 12.9 collective-permute-start.14
  1284.4 18.7 %all-to-all-start.32 = ((bf16[32,5,2048]{2,1,0:T(8,128)(2,1)}), bf16[32,5,2048]{2,1,0:T(8,128)(2,1)}, u32[]{:S(2)}, u32[]{:S(2)}) async-start(bf16[32,5,2048]{2,1,0:T(8,128)(2,1)} %select_n.1565), calls=%async_computation.32 | async-start | bytes 2097152 | tf_op jit(solution)/shard_map/all_to_all | solution.py:146
  1311.1 18.7 %all-to-all-start.33 = ((bf16[32,5,2048]{2,1,0:T(8,128)(2,1)}), bf16[32,5,2048]{2,1,0:T(8,128)(2,1)}, u32[]{:S(2)}, u32[]{:S(2)}) async-start(bf16[32,5,2048]{2,1,0:T(8,128)(2,1)} %copy.336), calls=%async_computation.33 | async-start | bytes 2097152 | tf_op jit(solution)/shard_map/all_to_all | solution.py:161
  1339.5 12.6 collective-permute-start.15
  1360.5 19.1 %all-to-all-start.34 = ((bf16[32,5,2048]{2,1,0:T(8,128)(2,1)}), bf16[32,5,2048]{2,1,0:T(8,128)(2,1)}, u32[]{:S(2)}, u32[]{:S(2)}) async-start(bf16[32,5,2048]{2,1,0:T(8,128)(2,1)} %select_n.1573), calls=%async_computation.34 | async-start | bytes 2097152 | tf_op jit(solution)/shard_map/all_to_all | solution.py:146
  1387.5 18.7 %all-to-all-start.35 = ((bf16[32,5,2048]{2,1,0:T(8,128)(2,1)}), bf16[32,5,2048]{2,1,0:T(8,128)(2,1)}, u32[]{:S(2)}, u32[]{:S(2)}) async-start(bf16[32,5,2048]{2,1,0:T(8,128)(2,1)} %copy.341), calls=%async_computation.35 | async-start | bytes 2097152 | tf_op jit(solution)/shard_map/all_to_all | solution.py:161
  1406.3 40.5 %all-to-all-start.21 = ((bf16[32,5,2048]{2,1,0:T(8,128)(2,1)}), bf16[32,5,2048]{2,1,0:T(8,128)(2,1)}, u32[]{:S(2)}, u32[]{:S(2)}) async-start(bf16[32,5,2048]{2,1,0:T(8,128)(2,1)} %bitcast.1840), calls=%async_computation.21 | async-start | bytes 2097152 | tf_op jit(solution)/shard_map/all_to_all | solution.py:106
  1424.7 13.7 collective-permute-start.16
  1446.8 23.8 %all-to-all-start.36 = ((bf16[32,5,2048]{2,1,0:T(8,128)(2,1)}), bf16[32,5,2048]{2,1,0:T(8,128)(2,1)}, u32[]{:S(2)}, u32[]{:S(2)}) async-start(bf16[32,5,2048]{2,1,0:T(8,128)(2,1)} %select_n.1581), calls=%async_computation.36 | async-start | bytes 2097152 | tf_op jit(solution)/shard_map/all_to_all | solution.py:146
  1478.6 18.7 %all-to-all-start.37 = ((bf16[32,5,2048]{2,1,0:T(8,128)(2,1)}), bf16[32,5,2048]{2,1,0:T(8,128)(2,1)}, u32[]{:S(2)}, u32[]{:S(2)}) async-start(bf16[32,5,2048]{2,1,0:T(8,128)(2,1)} %copy.346), calls=%async_computation.37 | async-start | bytes 2097152 | tf_op jit(solution)/shard_map/all_to_all | solution.py:161
  1506.9 9.4 collective-permute-start.17
  1525.3 18.7 %all-to-all-start.38 = ((bf16[32,5,2048]{2,1,0:T(8,128)(2,1)}), bf16[32,5,2048]{2,1,0:T(8,128)(2,1)}, u32[]{:S(2)}, u32[]{:S(2)}) async-start(bf16[32,5,2048]{2,1,0:T(8,128)(2,1)} %select_n.1589), calls=%async_computation.38 | async-start | bytes 2097152 | tf_op jit(solution)/shard_map/all_to_all | solution.py:146
  1552.3 18.7 %all-to-all-start.39 = ((bf16[32,5,2048]{2,1,0:T(8,128)(2,1)}), bf16[32,5,2048]{2,1,0:T(8,128)(2,1)}, u32[]{:S(2)}, u32[]{:S(2)}) async-start(bf16[32,5,2048]{2,1,0:T(8,128)(2,1)} %copy.351), calls=%async_computation.39 | async-start | bytes 2097152 | tf_op jit(solution)/shard_map/all_to_all | solution.py:161
  1580.7 12.5 collective-permute-start.18
  1601.6 19.4 %all-to-all-start.40 = ((bf16[32,5,2048]{2,1,0:T(8,128)(2,1)}), bf16[32,5,2048]{2,1,0:T(8,128)(2,1)}, u32[]{:S(2)}, u32[]{:S(2)}) async-start(bf16[32,5,2048]{2,1,0:T(8,128)(2,1)} %select_n.1597), calls=%async_computation.40 | async-start | bytes 2097152 | tf_op jit(solution)/shard_map/all_to_all | solution.py:146
  1628.9 20.5 %all-to-all-start.41 = ((bf16[32,5,2048]{2,1,0:T(8,128)(2,1)}), bf16[32,5,2048]{2,1,0:T(8,128)(2,1)}, u32[]{:S(2)}, u32[]{:S(2)}) async-start(bf16[32,5,2048]{2,1,0:T(8,128)(2,1)} %copy.356), calls=%async_computation.41 | async-start | bytes 2097152 | tf_op jit(solution)/shard_map/all_to_all | solution.py:161
  1659.1 6.2 collective-permute-start.19
  1673.7 22.3 %all-to-all-start.42 = ((bf16[32,5,2048]{2,1,0:T(8,128)(2,1)}), bf16[32,5,2048]{2,1,0:T(8,128)(2,1)}, u32[]{:S(2)}, u32[]{:S(2)}) async-start(bf16[32,5,2048]{2,1,0:T(8,128)(2,1)} %select_n.1605), calls=%async_computation.42 | async-start | bytes 2097152 | tf_op jit(solution)/shard_map/all_to_all | solution.py:146
  1704.0 19.2 %all-to-all-start.43 = ((bf16[32,5,2048]{2,1,0:T(8,128)(2,1)}), bf16[32,5,2048]{2,1,0:T(8,128)(2,1)S(1)}, u32[]{:S(2)}, u32[]{:S(2)}) async-start(bf16[32,5,2048]{2,1,0:T(8,128)(2,1)} %copy.361), calls=%async_computation.43 | async-start | bytes 2097152 | tf_op jit(solution)/shard_map/all_to_all | solution.py:161
  (124 other events, 1691.9 us)
where the time goes:
time: 1750 us; the launch traced here: 1730 us
  waiting for transfers between devices  570 us (33%)
  local copies, waits for them, and re-layouts  402 us (23%)
  other arithmetic  285 us (16%)
  starting transfers between devices  268 us (15%)
  matrix products  100 us (6%)
  blocking collectives  96.9 us (6%)
    all_to_all x11, waiting for transfers between devices, shards(): lax.all_to_all(sent, 'expert', split_axis=0, concat_axis=0, tiled=True)  151 us
    all_to_all x11, waiting for transfers between devices, shards(): lax.all_to_all(result.reshape(width, exp_dev * capacity, model), 'expert'...  126 us
    all_to_all x11, waiting for transfers between devices, shards(): lax.all_to_all(grad_rows, 'expert', split_axis=0, concat_axis=0, tiled=True)  114 us
    all_to_all x11, waiting for transfers between devices, shards(): lax.all_to_all(grads_sent, 'expert', split_axis=0, concat_axis=0, tiled=T...  109 us
    dynamic_update_slice x65, other arithmetic, put_slice(): lax.dynamic_update_index_in_dim(store, jnp.where(valid, value, older), sa...  103 us
    psum x1, blocking collectives, shards(): total = lax.psum(local_total, 'expert')  96.9 us
    ppermute x20, waiting for transfers between devices, shifted(): return lax.ppermute(value, axis, pairs)  69.8 us
    dynamic_slice x56, local copies, waits for them, and re-layouts, put_slice(): older = lax.dynamic_index_in_dim(store, safe, 0, keepdims=False)  63.5 us
  transfers between devices with their start and end apart: 64, of which 53 were waited for; matrix products, arithmetic and copies ran while one was open for 16% of the time, Pallas kernels for 0%

commit v1 on v0

v1 whole, which is shorter than its diff:
```python
import functools

import jax
import jax.numpy as jnp
from jax import lax
from jax.experimental import pallas as pl
from jax.experimental.pallas import tpu as pltpu
from jax.sharding import PartitionSpec as P

EPS = 1e-06
MESH = pl.DeviceIdType.MESH
BF = jnp.bfloat16
F32 = jnp.float32

PEERS = 32
CAP = 5
ROWS = PEERS * CAP
TOK = 16
TOP = 8
MICRO = 8
OWN = 4
D = 2048
FF = 768
SUB = 16
PAIRS = TOK * TOP
TAB = 384


def kernel(
    tok_hbm, cot_hbm, up_hbm, dn_hbm, it_hbm, ft_hbm, rloc_hbm, rw,
    lo_hbm, ig_hbm, gu_hbm,
    wup, wdn, rows, pre, gp, recv_a, recv_b, recv_d, send_a, send_b, work, nrm, gb, act, lay,
    gpart, grecv, xbuf, gbuf, itv, ftv, its, fts, rsum,
    wsem, wssem, tsem, tssem, ssem_t, rsem, rssem, asem, bsem, dsem, esem, ssa, ssb,
    insem, xsem, gsem, xs, osem, orsem, ossem, gusem, gssem,
):
    sec = lax.axis_index("section")
    me = lax.axis_index("expert")
    chip = sec // 2
    core = lax.rem(sec, 2)
    other = chip * 2 + (1 - core)
    across = (1 - chip) * 2 + core
    diag = (1 - chip) * 2 + (1 - core)

    pltpu.make_async_copy(up_hbm, wup.at[core], wsem.at[core, 0]).start()
    pltpu.make_async_copy(dn_hbm, wdn.at[core], wsem.at[core, 1]).start()
    pltpu.make_async_copy(it_hbm, itv.at[sec], tsem.at[0, sec]).start()
    pltpu.make_async_copy(ft_hbm, ftv.at[sec], tsem.at[1, sec]).start()

    def load_tokens(j, _):
        @pl.when(chip == 0)
        def _():
            pltpu.make_async_copy(tok_hbm.at[2 * j + core], xbuf.at[j, 0], insem.at[j]).start()

        @pl.when(chip == 1)
        def _():
            pltpu.make_async_copy(cot_hbm.at[2 * j + core], gbuf.at[j, 2], insem.at[j]).start()

        return 0

    lax.fori_loop(0, OWN, load_tokens, 0)

    barrier = pltpu.get_barrier_semaphore()

    def greet(i, _):
        p = lax.rem(me + 1 + i, PEERS)

        @pl.when(p != me)
        def _():
            pl.semaphore_signal(barrier, inc=1, device_id=(sec, p), device_id_type=MESH)

        pl.semaphore_signal(barrier, inc=1, device_id=(across, p), device_id_type=MESH)
        return 0

    lax.fori_loop(0, PEERS, greet, 0)
    pl.semaphore_signal(barrier, inc=1, device_id=(other, me), device_id_type=MESH)
    pl.semaphore_signal(barrier, inc=1, device_id=(diag, me), device_id_type=MESH)
    pl.semaphore_wait(barrier, 2 * PEERS + 1)

    for n, far in enumerate((other, across, diag)):
        pltpu.make_async_remote_copy(
            it_hbm, itv.at[sec], tssem.at[0, n], tsem.at[0, sec], device_id=(far, me), device_id_type=MESH
        ).start()
        pltpu.make_async_remote_copy(
            ft_hbm, ftv.at[sec], tssem.at[1, n], tsem.at[1, sec], device_id=(far, me), device_id_type=MESH
        ).start()

    @pl.when(chip == 1)
    def _():
        pltpu.make_async_copy(rloc_hbm, rsum.at[me], rsem).start()

        def send_sum(i, _):
            p = lax.rem(me + 1 + i, PEERS)
            pltpu.make_async_remote_copy(
                rloc_hbm, rsum.at[me], rssem, rsem, device_id=(sec, p), device_id_type=MESH
            ).start()
            return 0

        lax.fori_loop(0, PEERS - 1, send_sum, 0)

    w_up_far = pltpu.make_async_remote_copy(
        up_hbm, wup.at[core], wssem.at[0], wsem.at[core, 0], device_id=(other, me), device_id_type=MESH
    )
    w_dn_far = pltpu.make_async_remote_copy(
        dn_hbm, wdn.at[core], wssem.at[1], wsem.at[core, 1], device_id=(other, me), device_id_type=MESH
    )
    w_up_far.start()
    w_dn_far.start()

    def tables_in(n, _):
        pltpu.make_async_copy(itv.at[n], itv.at[n], tsem.at[0, n]).wait()
        pltpu.make_async_copy(ftv.at[n], ftv.at[n], tsem.at[1, n]).wait()
        return 0

    lax.fori_loop(0, 4, tables_in, 0)
    c1 = pltpu.make_async_copy(itv, its, ssem_t.at[0])
    c2 = pltpu.make_async_copy(ftv, fts, ssem_t.at[1])
    c1.start()
    c2.start()
    c1.wait()
    c2.wait()

    def wait_weights(q):
        pltpu.make_async_copy(wup.at[q], wup.at[q], wsem.at[q, 0]).wait()
        pltpu.make_async_copy(wdn.at[q], wdn.at[q], wsem.at[q, 1]).wait()

    def dispatch(j, layer, recv, sem, scaled):
        here = layer // 2 == chip
        target = (layer // 2) * 2 + core
        unit = lax.rem(layer, 2) * OWN + j
        m = 2 * j + core

        def one(i, _):
            p = lax.rem(me + 1 + i, PEERS)
            for r in range(CAP):
                at = PAIRS + p * CAP + r
                row = nrm[its[layer, m, at]]
                if scaled:
                    row = (row.astype(F32) * fts[layer, m, at]).astype(BF)
                send_a[j, p, r] = row

            @pl.when(jnp.logical_not(jnp.logical_and(here, p == me)))
            def _():
                pltpu.make_async_remote_copy(
                    send_a.at[j, p], recv.at[unit, me], ssa.at[j], sem.at[unit],
                    device_id=(target, p), device_id_type=MESH,
                ).start()

            return 0

        lax.fori_loop(0, PEERS, one, 0)

        @pl.when(here)
        def _():
            recv[unit, me] = send_a[j, me]

    def wait_blocks(buffer, sem, far):
        most = buffer.at[pl.ds(0, PEERS - 1)]
        if far is False:
            pltpu.make_async_copy(most, most, sem).wait()
            return

        @pl.when(far)
        def _():
            pltpu.make_async_copy(buffer, buffer, sem).wait()

        @pl.when(jnp.logical_not(far))
        def _():
            pltpu.make_async_copy(most, most, sem).wait()

    def wait_dispatch(j, far):
        wait_blocks(send_a.at[j], ssa.at[j], far)

    def normed(value):
        v = value.astype(F32)
        mean = jnp.sum(v * v, axis=(0, 1), keepdims=True) * (1.0 / D)
        return (v * lax.rsqrt(mean + EPS)).astype(BF)

    def first_forward(j, _):
        pltpu.make_async_copy(xbuf.at[j, 0], xbuf.at[j, 0], insem.at[j]).wait()

        def one(t, _):
            nrm[t] = normed(xbuf[j, 0, t])
            return 0

        lax.fori_loop(0, TOK, one, 0, unroll=4)
        dispatch(j, 0, recv_a, asem, False)
        return 0

    def first_backward(j, _):
        pltpu.make_async_copy(gbuf.at[j, 2], gbuf.at[j, 2], insem.at[j]).wait()
        total = jnp.sum(rsum[...], axis=0)
        inverse = (MICRO * TOK * PEERS) / total
        m = 2 * j + core

        def one(t, _):
            factor = rw[m, t] * inverse[0:1, :]
            g = (gbuf[j, 2, t].astype(F32) * factor).astype(BF)
            gbuf[j, 2, t] = g
            nrm[t] = g
            return 0

        lax.fori_loop(0, TOK, one, 0, unroll=4)
        dispatch(j, 3, recv_d, dsem, True)
        return 0

    @pl.when(chip == 0)
    def _():
        lax.fori_loop(0, 2, first_forward, 0)

    @pl.when(chip == 1)
    def _():
        pltpu.make_async_copy(rsum, rsum, rsem).wait()
        lax.fori_loop(0, OWN, first_backward, 0)
        pltpu.make_async_copy(rsum.at[pl.ds(0, PEERS - 1)], rsum.at[pl.ds(0, PEERS - 1)], rssem).wait()

    wait_weights(0)

    def flatten(recv, unit, dst, *lead):
        for n in range(PEERS):
            lay[pl.ds(n * CAP * SUB, CAP * SUB), :] = (
                recv[unit, n].astype(F32).reshape(CAP * SUB, 128)
            )
        for n in range(ROWS // SUB):
            for b in range(SUB):
                part = lay[pl.ds(n * SUB * SUB + b, SUB, stride=SUB), :]
                if lead:
                    q, start = lead
                    dst[q, pl.ds(pl.multiple_of(start + n * SUB, SUB), SUB), pl.ds(b * 128, 128)] = part.astype(BF)
                else:
                    dst[pl.ds(n * SUB, SUB), pl.ds(b * 128, 128)] = part.astype(BF)

    def put_back(n, tile):
        for h in range(2):
            lay[pl.ds(2 * n + h, ROWS, stride=SUB), :] = tile[:, h * 128:(h + 1) * 128]

    def give_back(slot, unit, sem, again):
        @pl.when(again)
        def _():
            pltpu.make_async_copy(
                send_b.at[slot, pl.ds(0, PEERS - 1)], send_b.at[slot, pl.ds(0, PEERS - 1)], ssb.at[slot]
            ).wait()

        def one(i, _):
            p = lax.rem(me + 1 + i, PEERS)
            at = pl.multiple_of(p * (CAP * SUB), CAP * SUB)
            send_b[slot, p] = lay[pl.ds(at, CAP * SUB), :].reshape(CAP, SUB, 128).astype(BF)

            @pl.when(p != me)
            def _():
                pltpu.make_async_remote_copy(
                    send_b.at[slot, p], recv_b.at[unit, me], ssb.at[slot], sem.at[unit],
                    device_id=(sec, p), device_id_type=MESH,
                ).start()

            return 0

        lax.fori_loop(0, PEERS, one, 0)
        recv_b[unit, me] = send_b[slot, me]

    def expert_forward(j, q, slot, again):
        unit = q * OWN + j
        start = pl.multiple_of(j * ROWS, ROWS)
        wait_blocks(recv_a.at[unit], asem.at[unit], jnp.logical_and(chip == 1, q == 0))
        flatten(recv_a, unit, rows, q, start)
        span = pl.ds(start, ROWS)
        for n in range(FF // 256):
            cols = pl.ds(n * 256, 256)
            v = jnp.dot(rows[q, span, :], wup[q, :, cols], preferred_element_type=F32)
            pre[q, span, cols] = v
            act[:, cols] = (v * jax.nn.sigmoid(v)).astype(BF)
        for n in range(D // 256):
            put_back(n, jnp.dot(act[...], wdn[q, :, pl.ds(n * 256, 256)], preferred_element_type=F32))
        give_back(slot, unit, bsem, again)

    contract_last = (((1,), (1,)), ((), ()))

    def expert_backward(j, q, slot):
        unit = q * OWN + j
        start = pl.multiple_of(j * ROWS, ROWS)
        wait_blocks(recv_d.at[unit], dsem.at[unit], jnp.logical_and(chip == 0, q == 1))
        flatten(recv_d, unit, gb)
        span = pl.ds(start, ROWS)
        for n in range(FF // 256):
            cols = pl.ds(n * 256, 256)
            v = lax.dot_general(gb[...], wdn[q, cols, :], contract_last, preferred_element_type=F32)
            h = pre[q, span, cols]
            s = jax.nn.sigmoid(h)
            gp[q, span, cols] = (v * (s * (1.0 + h * (1.0 - s)))).astype(BF)
        for n in range(D // 256):
            put_back(
                n,
                lax.dot_general(
                    gp[q, span, :], wup[q, pl.ds(n * 256, 256), :], contract_last, preferred_element_type=F32
                ),
            )
        give_back(slot, unit, esem, True)

    def copy_out(kind, j, q, src, dst_hbm):
        m = 2 * j + core

        @pl.when(q == core)
        def _():
            pltpu.make_async_copy(src, dst_hbm.at[m], osem.at[kind, j]).start()

        @pl.when(q != core)
        def _():
            pltpu.make_async_remote_copy(
                src, dst_hbm.at[m], ossem.at[kind, j], orsem.at[kind, j],
                device_id=(other, me), device_id_type=MESH,
            ).start()

    def home_forward(j, q):
        unit = q * OWN + j
        layer = 2 * chip + q
        m = 2 * j + core

        @pl.when(jnp.logical_and(chip == 1, q == 0))
        def _():
            pltpu.make_async_copy(xbuf.at[j, 0], xbuf.at[j, 0], xsem.at[j]).wait()

        wait_blocks(recv_b.at[unit], bsem.at[unit], False)
        work[...] = recv_b[unit].reshape(ROWS, SUB, 128)

        def one(t, _):
            total = xbuf[j, q, t].astype(F32)
            for n in range(TOP):
                total += fts[layer, m, t * TOP + n] * work[its[layer, m, t * TOP + n]].astype(F32)
            out = total.astype(BF)
            xbuf[j, q + 1, t] = out
            nrm[t] = normed(out)
            return 0

        lax.fori_loop(0, TOK, one, 0, unroll=4)

        @pl.when(jnp.logical_not(jnp.logical_and(chip == 1, q == 1)))
        def _():
            wait_dispatch(j, False)
            dispatch(j, layer + 1, recv_a, asem, False)

        @pl.when(jnp.logical_and(chip == 0, q == 1))
        def _():
            pltpu.make_async_remote_copy(
                xbuf.at[j, 2], xbuf.at[j, 0], xs.at[j], xsem.at[j],
                device_id=(across, me), device_id_type=MESH,
            ).start()

        copy_out(0, j, q, xbuf.at[j, q + 1], lo_hbm)

    def home_backward(j, q):
        unit = q * OWN + j
        layer = 2 * chip + q
        m = 2 * j + core

        @pl.when(jnp.logical_and(chip == 0, q == 1))
        def _():
            pltpu.make_async_copy(gbuf.at[j, 2], gbuf.at[j, 2], gsem.at[j]).wait()

        wait_blocks(recv_b.at[unit], esem.at[unit], False)
        work[...] = recv_b[unit].reshape(ROWS, SUB, 128)

        def one(t, _):
            grad = work[its[layer, m, t * TOP]].astype(F32)
            for n in range(1, TOP):
                grad += work[its[layer, m, t * TOP + n]].astype(F32)
            x = xbuf[j, q, t].astype(F32)
            scale = lax.rsqrt(jnp.sum(x * x, axis=(0, 1), keepdims=True) * (1.0 / D) + EPS)
            inner = jnp.sum(grad * x, axis=(0, 1), keepdims=True) * (1.0 / D)
            g = gbuf[j, q + 1, t].astype(F32)
            out = (g + (scale * grad - x * (scale * scale * scale) * inner)).astype(BF)
            gbuf[j, q, t] = out
            nrm[t] = out
            return 0

        lax.fori_loop(0, TOK, one, 0, unroll=4)

        @pl.when(jnp.logical_not(jnp.logical_and(chip == 0, q == 0)))
        def _():
            wait_dispatch(j, chip == 0)
            dispatch(j, layer - 1, recv_d, dsem, True)

        @pl.when(jnp.logical_and(chip == 1, q == 0))
        def _():
            pltpu.make_async_remote_copy(
                gbuf.at[j, 0], gbuf.at[j, 2], xs.at[j], gsem.at[j],
                device_id=(across, me), device_id_type=MESH,
            ).start()

        copy_out(1, j, q, gbuf.at[j, q], ig_hbm)

    def forward_step(step, _):
        pair, q = step // 2, lax.rem(step, 2)

        @pl.when(step == 1)
        def _():
            wait_weights(1)

        def run(i, _):
            expert_forward(2 * pair + i, q, i, step > 0)
            return 0

        lax.fori_loop(0, 2, run, 0)

        @pl.when(jnp.logical_and(step == 0, chip == 0))
        def _():
            lax.fori_loop(2, OWN, first_forward, 0)

        def close(i, _):
            home_forward(2 * pair + i, q)
            return 0

        lax.fori_loop(0, 2, close, 0)
        return 0

    lax.fori_loop(0, 4, forward_step, 0)

    def weight_grad(q):
        def one(n, _):
            at = pl.multiple_of(n * 256, 256)
            gpart[q, pl.ds(at, 256), :] = lax.dot_general(
                rows[q, :, pl.ds(at, 256)], gp[q], (((0,), (0,)), ((), ())), preferred_element_type=F32
            ).astype(BF)
            return 0

        lax.fori_loop(0, D // 256, one, 0)

    def backward_step(step, _):
        pair, q = step // 2, 1 - lax.rem(step, 2)

        def run(i, _):
            expert_backward(2 * pair + i, q, i)
            return 0

        lax.fori_loop(0, 2, run, 0)

        @pl.when(step >= 2)
        def _():
            weight_grad(q)

            @pl.when(q != core)
            def _():
                pltpu.make_async_remote_copy(
                    gpart.at[q], grecv, gssem, gusem.at[0], device_id=(other, me), device_id_type=MESH
                ).start()

        def close(i, _):
            home_backward(2 * pair + i, q)
            return 0

        lax.fori_loop(0, 2, close, 0)
        return 0

    lax.fori_loop(0, 4, backward_step, 0)

    pltpu.make_async_copy(grecv, grecv, gusem.at[0]).wait()

    def add(n, _):
        at = pl.ds(pl.multiple_of(n * 128, 128), 128)
        gpart[core, at, :] = (gpart[core, at, :].astype(F32) + grecv[at, :].astype(F32)).astype(BF)
        return 0

    lax.fori_loop(0, D // 128, add, 0)
    last = pltpu.make_async_copy(gpart.at[core], gu_hbm, gusem.at[1])
    last.start()

    def drain(j, _):
        wait_dispatch(j, chip == 1)
        pltpu.make_async_copy(xbuf.at[j, 0], xbuf.at[j, 0], xs.at[j]).wait()
        for kind in range(2):
            for sem in (osem, orsem, ossem):
                pltpu.make_async_copy(xbuf.at[j, 0], xbuf.at[j, 0], sem.at[kind, j]).wait()
        return 0

    lax.fori_loop(0, OWN, drain, 0)
    for slot in range(2):
        pltpu.make_async_copy(
            send_b.at[slot, pl.ds(0, PEERS - 1)], send_b.at[slot, pl.ds(0, PEERS - 1)], ssb.at[slot]
        ).wait()
    pltpu.make_async_copy(grecv, grecv, gssem).wait()
    w_up_far.wait_send()
    w_dn_far.wait_send()
    for n in range(3):
        pltpu.make_async_copy(itv.at[0], itv.at[0], tssem.at[0, n]).wait()
        pltpu.make_async_copy(ftv.at[0], ftv.at[0], tssem.at[1, n]).wait()
    last.wait()


def tables(routes, combine):
    route = routes.reshape(MICRO, PAIRS)
    coef = combine.reshape(MICRO, PAIRS)
    place = jnp.arange(PAIRS, dtype=jnp.int32)
    same = (route[:, :, None] == route[:, None, :]) & (place[None, None, :] < place[None, :, None])
    slot = route * CAP + jnp.sum(same.astype(jnp.int32), axis=2)
    hit = slot[:, None, :] == jnp.arange(ROWS, dtype=jnp.int32)[None, :, None]
    token = jnp.sum(jnp.where(hit, (place // TOP)[None, None, :], 0), axis=2)
    weight = jnp.sum(jnp.where(hit, coef[:, None, :], 0.0), axis=2)
    rest = TAB - PAIRS - ROWS
    ints = jnp.concatenate([slot, token, jnp.zeros((MICRO, rest), jnp.int32)], axis=1)
    floats = jnp.concatenate([coef, weight, jnp.zeros((MICRO, rest), F32)], axis=1)
    return ints, floats


def shards(tokens, cotangent, reward_weight, routes, combine, w_up, w_down):
    ints, floats = tables(routes[0], combine[0])
    local = jnp.broadcast_to(jnp.sum(reward_weight), (8, 128))
    blocks = (MICRO, TOK, SUB, 128)
    exchange = (PEERS, CAP, SUB, 128)
    anywhere = pl.BlockSpec(memory_space=pl.ANY)
    dma = pltpu.SemaphoreType.DMA
    lo, ig, gu = pl.pallas_call(
        kernel,
        out_shape=(
            jax.ShapeDtypeStruct(blocks, BF),
            jax.ShapeDtypeStruct(blocks, BF),
            jax.ShapeDtypeStruct((D, FF), BF),
        ),
        in_specs=[anywhere] * 7 + [pl.BlockSpec(memory_space=pltpu.SMEM)],
        out_specs=(anywhere,) * 3,
        scratch_shapes=[
            pltpu.VMEM((2, D, FF), BF),
            pltpu.VMEM((2, FF, D), BF),
            pltpu.VMEM((2, OWN * ROWS, D), BF),
            pltpu.VMEM((2, OWN * ROWS, FF), F32),
            pltpu.VMEM((2, OWN * ROWS, FF), BF),
            pltpu.VMEM((2 * OWN,) + exchange, BF),
            pltpu.VMEM((2 * OWN,) + exchange, BF),
            pltpu.VMEM((2 * OWN,) + exchange, BF),
            pltpu.VMEM((OWN,) + exchange, BF),
            pltpu.VMEM((2,) + exchange, BF),
            pltpu.VMEM((ROWS, SUB, 128), BF),
            pltpu.VMEM((TOK, SUB, 128), BF),
            pltpu.VMEM((ROWS, D), BF),
            pltpu.VMEM((ROWS, FF), BF),
            pltpu.VMEM((ROWS * SUB, 128), F32),
            pltpu.VMEM((2, D, FF), BF),
            pltpu.VMEM((D, FF), BF),
            pltpu.VMEM((OWN, 3, TOK, SUB, 128), BF),
            pltpu.VMEM((OWN, 3, TOK, SUB, 128), BF),
            pltpu.VMEM((4, MICRO, TAB), jnp.int32),
            pltpu.VMEM((4, MICRO, TAB), F32),
            pltpu.SMEM((4, MICRO, TAB), jnp.int32),
            pltpu.SMEM((4, MICRO, TAB), F32),
            pltpu.VMEM((PEERS, 8, 128), F32),
            dma((2, 2)), dma((2,)), dma((2, 4)), dma((2, 3)), dma((2,)), dma, dma,
            dma((2 * OWN,)), dma((2 * OWN,)), dma((2 * OWN,)), dma((2 * OWN,)), dma((OWN,)), dma((2,)),
            dma((OWN,)), dma((OWN,)), dma((OWN,)), dma((OWN,)),
            dma((2, OWN)), dma((2, OWN)), dma((2, OWN)), dma((2,)), dma,
        ],
        compiler_params=pltpu.CompilerParams(
            collective_id=0, has_side_effects=True, vmem_limit_bytes=62 * 1024 * 1024
        ),
        cost_estimate=pl.CostEstimate(
            flops=2 * 5 * MICRO * ROWS * D * FF, bytes_accessed=16 * 2**20, transcendentals=2 * MICRO * ROWS * FF
        ),
    )(
        tokens.reshape(blocks), cotangent.reshape(blocks), w_up[0, 0], w_down[0, 0], ints, floats, local, reward_weight
    )
    whole = (1, MICRO, TOK, D)
    return lo.reshape(whole), ig.reshape(whole), gu[None, None]


def solution(mesh):
    return jax.shard_map(
        shards,
        mesh=mesh,
        in_specs=(
            P(None, "expert", None),
            P(None, "expert", None),
            P(None, "expert"),
            P("section", None, "expert", None),
            P("section", None, "expert", None),
            P("section", "expert", None, None),
            P("section", "expert", None, None),
        ),
        out_specs=(
            P("section", None, "expert", None),
            P("section", None, "expert", None),
            P("section", "expert", None, None),
        ),
        check_vma=False,
    )
```

time: 1750 us -> 427 us (0.24); the launches traced: 1730 us -> 426 us
  waiting for transfers between devices: 570 us -> 0 us
  Pallas kernels: 0 us -> 407 us
  local copies, waits for them, and re-layouts: 402 us -> 15 us
  other arithmetic: 285 us -> 3.61 us
  starting transfers between devices: 268 us -> 0 us
  matrix products: 100 us -> 0 us
  blocking collectives: 96.9 us -> 0 us
    all_to_all x44 -> x0, waiting for transfers between devices: 500 us -> none  [the longest x11 151 us: shards(): lax.all_to_all(sent, 'expert', split_axis=0, concat_axis=0, tiled=True)]
    pallas_call x0 -> x1, Pallas kernels: none -> 407 us  [shards(): pl.pallas_call(kernel, out_shape=(jax.ShapeDtypeStruct(blocks, BF), jax.S...]
    all_to_all x44 -> x0, starting transfers between devices: 237 us -> none  [the longest x11 63.5 us: shards(): lax.all_to_all(sent, 'expert', split_axis=0, concat_axis=0, tiled=True)]
    dynamic_update_slice x65 -> x0, other arithmetic: 103 us -> none  [put_slice(): lax.dynamic_update_index_in_dim(store, jnp.where(valid, value, older), sa...]
    dot_general x33 -> x0, matrix products: 100 us -> none  [the longest x8 35.9 us: expert_backward(): jnp.einsum('sjcd,jfd->sjcf', grads_blocks, down_local, preferred_element_...]
    psum x1 -> x0, blocking collectives: 96.9 us -> none  [shards(): total = lax.psum(local_total, 'expert')]
    gather x22 -> x0, local copies, waits for them, and re-layouts: 73.9 us -> none  [the longest x11 38.2 us: shards(): rows = returned.reshape(experts * capacity, model)[slot].astype(jnp.float32)]
    dynamic_slice x91 -> x0, local copies, waits for them, and re-layouts: 72.6 us -> none  [the longest x56 63.5 us: put_slice(): older = lax.dynamic_index_in_dim(store, safe, 0, keepdims=False)]
  transfers between devices with their start and end apart: 64 -> 0, of which waited for: 53 -> 0; matrix products, arithmetic and copies ran while one was open for 16% -> 0% of each run, Pallas kernels for 0% -> 0%
where the time goes in v1:
time: 427 us; the launch traced here: 426 us
  Pallas kernels  407 us (95%)
  local copies, waits for them, and re-layouts  15 us (4%)
    pallas_call x1, Pallas kernels, shards(): pl.pallas_call(kernel, out_shape=(jax.ShapeDtypeStruct(blocks, BF), jax.S...  407 us
    unnamed x5, local copies, waits for them, and re-layouts  9.31 us

profile of v1, /device:TPU:0, one launch (start us, length us, event | category | flops | bytes accessed | tf_op | source)
XLA Modules:
  0.0 426.2 jit_solution(7586176739474978634)
XLA Ops:
  0.6 1.3 reduce_sum.39
  1.9 0.1 pad.2.clone
  2.0 0.1 pad.5.clone
  2.1 1.2 broadcast_in_dim.47.rloc_hbm
  3.3 0.8 copy.14
  4.2 0.1 reshape_squeeze.6
  4.3 0.4 convert_reduce_fusion
  4.7 0.4 select_reduce_fusion.1
  5.0 0.6 add_add_fusion.it_hbm
  5.6 0.8 copy.15
  6.5 0.1 reshape_squeeze.7
  6.6 0.4 select_reduce_fusion
  6.9 0.6 maximum_maximum_fusion.ft_hbm
  7.5 1.9 copy.16
  9.5 1.9 copy.17
  11.4 406.9 %shard_map.94 = (bf16[8,16,16,128]{3,2,1,0:T(8,128)(2,1)}, bf16[8,16,16,128]{3,2,1,0:T(8,128)(2,1)}, bf16[2048,768]{1,0:T(8,128)(2,1)}) custom-call(bf16[8,16,16,128]{3,2,1,0:T(8,128)(2,1)} %bitcast.22, bf16[8,16,16,128]{3,2,1,0:T(8,128)(2,1)} %bitcast.23, bf16[2048,768]{1,0:T(8,128)(2,1)} %bitcast.24, bf16[768,2048]{1,0:T(8,128)(2,1)} %bitcast.25, ...), custom_call_target="tpu_custom_call" | custom-call | flops 20132659200 | bytes 16777216 | tf_op jit(solution)/shard_map/pallas_call | solution.py:510
  418.3 2.1 reshape.59
  420.4 2.1 reshape.60
  422.5 3.8 copy.19
  (5 shorter events, 0.0 us)
